TPU v7x, 128 devices: a whole 4x4x4 slice. The times are simulated.
128 devices in a mesh: span: 8 (over x_hi, z), seq: 16 (over x_lo, y, core).
Axes of the slice: x: 4 (x_hi: 2, x_lo: 2; x = x_hi * 2 + x_lo), y: 4, z: 4, core: 2. Of those that a mesh axis runs over, the one named last changes fastest.
Arguments:
- projected: bfloat16 [8, 2048, 8192], P('span', 'seq'), may hold values from -7 to 7
- cache_kv: bfloat16 [2048, 2, 1024], P('seq'), may hold values from -6 to 6
- levels: int32 [8], P('span'), may hold values from 0 to 15
- cache_blocks: int32 [8], P('span'), may hold values from 1 to 16, as said below
- gate_table: float32 [16, 6144], P(None, 'seq'), may hold values from 0.1 to 1.9
Outputs:
- gated: bfloat16 [8, 2048, 6144], P('span', 'seq')
Inputs may be any that keep to these rules, and one draw needn't show every extreme that they name: `cache_blocks`: nondecreasing along the spans; the last span's entry equals 16.
All inputs are finite; a program needn't handle non-finite values.
Results may differ from a plain program's by a relative error of at most 0.0095.
Values may be sent and summed in bfloat16 or wider, within the bound.
A program may use at most 128 MiB of HBM per device.

v0:
```python
import functools

import jax
import jax.numpy as jnp
from jax import lax
from jax.experimental import pallas as pl
from jax.experimental.pallas import tpu as pltpu
from jax.sharding import PartitionSpec as P

MODEL_WIDTH = 6144
HEAD_DIM = 128
KV_WIDTH = 1024
SPANS = 8
SEQ = 16
TOK = 128
HEADS = 3
QW = HEADS * HEAD_DIM
SPAN_TOKENS = 2048
HALF = SPAN_TOKENS // 2
CHUNK = 512
BQ = 512
QBLOCKS = 12
SUB = 512
NEGATIVE = -1e30
MASKED = 1e30
SCALE = HEAD_DIM ** -0.5 * 1.4426950408889634
OWN, CACHE, NEAR, FAR = range(4)
MESH = pl.DeviceIdType.MESH

CACHE_STEP = 7
NEAR_STEPS = (6, 11)
FAR_STEPS = (17, 22)


def kernel(
    x, cache, levels, blocks, gate, out,
    kv, vt, qin, qt, acc, top, total, s0, s1, stage, gates,
    kv_send, kv_recv, local_sem, side_send, side_recv, pass_send, pass_recv,
    q_send, q_recv, out_send, out_recv, out_local,
):
    c = lax.axis_index("span")
    s = lax.axis_index("seq")
    chip = s // 2
    core = s % 2
    xlo = chip // 4
    y = chip % 4
    group = s // 4
    limit = blocks[0]
    windows = jnp.minimum(c, 2)
    ways = jnp.maximum(windows, 1)
    steps = 2 * QBLOCKS + QBLOCKS * windows
    beside = {"span": c, "seq": 2 * chip + (1 - core)}
    after = {"span": jnp.minimum(c + 1, SPANS - 1), "seq": s}

    barrier = pltpu.get_barrier_semaphore()
    for d in range(1, SEQ):
        pl.semaphore_signal(barrier, inc=1, device_id={"span": c, "seq": (s + d) % SEQ}, device_id_type=MESH)

    @pl.when(c > 0)
    def _():
        pl.semaphore_signal(barrier, inc=1, device_id={"span": jnp.maximum(c - 1, 0), "seq": s}, device_id_type=MESH)

    @pl.when(c < SPANS - 1)
    def _():
        pl.semaphore_signal(barrier, inc=1, device_id=after, device_id_type=MESH)

    pl.semaphore_wait(barrier, SEQ - 1 + jnp.where(c > 0, 1, 0) + jnp.where(c < SPANS - 1, 1, 0))

    def source(stream, which, head):
        if stream == OWN:
            return x.at[0, :, pl.ds(pl.multiple_of(MODEL_WIDTH + KV_WIDTH * which + HEAD_DIM * head, 128), HEAD_DIM)]
        return cache.at[:, pl.ds(pl.multiple_of(KV_WIDTH * which + HEAD_DIM * head, 128), HEAD_DIM)]

    def send_kv(stream):
        piece = pl.ds(pl.multiple_of(TOK * chip, TOK), TOK)
        for dx, dy in ((0, 1), (0, 3), (0, 2), (1, 0), (1, 1), (1, 3), (1, 2)):
            there = ((xlo + dx) % 2) * 4 + (y + dy) % 4
            for which in range(2):
                pltpu.make_async_remote_copy(
                    src_ref=source(stream, which, there),
                    dst_ref=kv.at[stream, core, which, piece],
                    send_sem=kv_send.at[stream],
                    recv_sem=kv_recv.at[stream, xlo],
                    device_id={"span": c, "seq": 2 * there + core},
                    device_id_type=MESH,
                ).start()
        for which in range(2):
            pltpu.make_async_copy(source(stream, which, chip), kv.at[stream, core, which, piece], local_sem.at[stream]).start()

    def group_at(turn):
        return ((group // 2 + turn // 2) % 2) * 2 + (group % 2 + turn % 2) % 2

    def send_q(turn):
        for e in range(4):
            there = 4 * group_at(turn) + (s % 4 + e) % 4
            wanted = x.at[0, :, pl.ds(pl.multiple_of(QW * there, 128), QW)]
            if turn == 0 and e == 0:
                pltpu.make_async_copy(wanted, qin.at[s], local_sem.at[2]).start()
            else:
                pltpu.make_async_remote_copy(
                    src_ref=wanted,
                    dst_ref=qin.at[s],
                    send_sem=q_send,
                    recv_sem=q_recv.at[group],
                    device_id={"span": c, "seq": there},
                    device_id_type=MESH,
                ).start()

    send_kv(OWN)
    send_q(0)
    send_q(1)
    send_q(2)
    send_kv(CACHE)
    send_q(3)

    def clear(i, unused):
        acc[i] = jnp.zeros((HEAD_DIM, BQ), jnp.float32)
        total[i] = jnp.zeros((8, BQ), jnp.float32)
        top[i] = jnp.full((8, BQ), NEGATIVE, jnp.float32)
        return unused

    lax.fori_loop(0, QBLOCKS, clear, 0)
    level_rows = lax.broadcasted_iota(jnp.int32, gate.shape, 0)
    chosen = jnp.sum(jnp.where(level_rows == levels[0], gate[...], 0.0), axis=0, keepdims=True)
    gates[...] = jnp.broadcast_to(chosen, gates.shape)

    def wait_bytes(ref, sem):
        pltpu.make_async_copy(ref, ref, sem).wait()

    def half_rows(part):
        return pl.ds(pl.multiple_of(CHUNK * part, CHUNK), CHUNK)

    def side_copy(stream, part):
        piece = kv.at[stream, core, :, half_rows(part)]
        return pltpu.make_async_remote_copy(
            src_ref=piece, dst_ref=piece, send_sem=side_send.at[stream, part], recv_sem=side_recv.at[stream, part],
            device_id=beside, device_id_type=MESH,
        )

    def pass_copy(stream, part):
        return pltpu.make_async_remote_copy(
            src_ref=kv.at[stream, core, :, half_rows(part)],
            dst_ref=kv.at[FAR if stream == NEAR else NEAR, core, :, half_rows(part)],
            send_sem=pass_send.at[stream // 2, part], recv_sem=pass_recv.at[stream // 2, part],
            device_id=after, device_id_type=MESH,
        )

    def take_kv(stream, first):
        part = xlo if first else 1 - xlo
        if first:
            wait_bytes(kv.at[stream, core, :, pl.ds(0, TOK)], local_sem.at[stream])
        rows = 3 * TOK if first else 4 * TOK
        wait_bytes(kv.at[stream, core, :, pl.ds(0, rows)], kv_recv.at[stream, part])
        side_copy(stream, part).start()
        if stream == OWN:
            @pl.when(c < SPANS - 1)
            def _():
                pass_copy(OWN, part).start()

    def take_window(stream, first):
        part = xlo if first else 1 - xlo
        wait_bytes(kv.at[stream, core, :, pl.ds(0, CHUNK)], pass_recv.at[0 if stream == NEAR else 1, part])
        side_copy(stream, part).start()
        if stream == NEAR:
            @pl.when(c < SPANS - 1)
            def _():
                pass_copy(NEAR, part).start()

    def take_side(stream):
        for part in range(2):
            wait_bytes(kv.at[stream, 1 - core, :, pl.ds(0, CHUNK)], side_recv.at[stream, part])
        for p in range(2):
            for b in range(0, HALF, 512):
                values = kv[stream, p, 1, pl.ds(b, 512), :]
                vt[stream, :, pl.ds(p * HALF + b, 512)] = jnp.transpose(values)

    def take_q(i):
        g = group_at(i // HEADS)

        @pl.when(i == 0)
        def _():
            wait_bytes(qin.at[0], local_sem.at[2])
            wait_bytes(qin.at[pl.ds(0, 3)], q_recv.at[g])

        @pl.when((i > 0) & (i % HEADS == 0))
        def _():
            wait_bytes(qin.at[pl.ds(0, 4)], q_recv.at[g])

        h = i % HEADS
        rows = qin[pl.ds(4 * g, 4), :, pl.ds(pl.multiple_of(h * HEAD_DIM, 128), HEAD_DIM)].reshape(BQ, HEAD_DIM)
        scaled = jnp.transpose(rows.astype(jnp.float32) * SCALE)
        high = scaled.astype(jnp.bfloat16)
        qt[i, pl.ds(0, 128), :] = high
        qt[i, pl.ds(128, 128), :] = (scaled - high.astype(jnp.float32)).astype(jnp.bfloat16)

    def place(t):
        late = t - 2 * QBLOCKS
        early = t < 2 * QBLOCKS
        stream = jnp.where(early, t // QBLOCKS, NEAR + late % ways)
        block = jnp.where(early, t % QBLOCKS, late // ways)
        return stream, block

    def masked(stream, p, piece):
        return jnp.where((stream == CACHE) & (2 * piece + p >= limit), MASKED, 0.0).astype(jnp.float32)

    def scores(t, into):
        stream, block = place(t)
        queries = qt[block]
        best = None
        for ch in range(SPAN_TOKENS // SUB):
            p, start = divmod(ch * SUB, HALF)
            keys = kv[stream, p, 0, pl.ds(start, SUB), :]
            part = jnp.dot(jnp.concatenate([keys, keys], axis=1), queries, preferred_element_type=jnp.float32)
            into[pl.ds(ch * SUB, SUB), :] = part
            for b in range(SUB // TOK):
                here = jnp.max(part[b * TOK:(b + 1) * TOK].reshape(TOK // 8, 8, BQ), axis=0)
                here = here - masked(stream, p, (start + b * TOK) // TOK)
                best = here if best is None else jnp.maximum(best, here)
        best = jnp.max(best, axis=0, keepdims=True)
        old = top[block, 0:1, :]
        return old, jnp.maximum(old, best)

    def arrivals(t):
        @pl.when(t < QBLOCKS)
        def _():
            take_q(t)

        @pl.when(t == CACHE_STEP)
        def _():
            take_kv(CACHE, True)
            take_kv(CACHE, False)

        for which, at in enumerate(NEAR_STEPS):
            @pl.when((t == at) & (c >= 1))
            def _(which=which):
                take_window(NEAR, which == 0)

        for which, at in enumerate(FAR_STEPS):
            @pl.when((t == at) & (c >= 2))
            def _(which=which):
                take_window(FAR, which == 0)

        @pl.when(t == QBLOCKS)
        def _():
            take_side(CACHE)

        @pl.when((t == 2 * QBLOCKS) & (c >= 1))
        def _():
            take_side(NEAR)

        @pl.when((t == 2 * QBLOCKS + 1) & (c >= 2))
        def _():
            take_side(FAR)

    def finish(block):
        summed = acc[block]
        whole = jnp.sum(total[block], axis=0, keepdims=True)
        square = jnp.mean(summed * summed, axis=0, keepdims=True)
        normed = summed * lax.rsqrt(square + 1e-06 * (whole * whole))
        h = block % HEADS
        g = group_at(block // HEADS)
        row = gates[0:1, pl.ds(pl.multiple_of(h * HEAD_DIM, 128), HEAD_DIM)]
        stage[block] = (jnp.transpose(normed) * row).astype(jnp.bfloat16)
        wanted = out.at[0, :, pl.ds(pl.multiple_of((HEADS * s + h) * HEAD_DIM, 128), HEAD_DIM)]
        for e in range(4):
            there = 4 * g + e
            held = stage.at[block, pl.ds(e * TOK, TOK)]

            @pl.when(there == s)
            def _():
                pltpu.make_async_copy(held, wanted, out_local).start()

            @pl.when(there != s)
            def _():
                pltpu.make_async_remote_copy(
                    src_ref=held, dst_ref=wanted, send_sem=out_send, recv_sem=out_recv,
                    device_id={"span": c, "seq": there}, device_id_type=MESH,
                ).start()

    def step(t, now, later, best):
        old, new = best
        stream, block = place(t)
        top[block, 0:1, :] = new
        following = jnp.minimum(t + 1, steps - 1)

        @pl.when(t + 1 < steps)
        def _():
            arrivals(t + 1)

        best = scores(following, later)
        factor = jnp.exp2(old - new)
        update = None
        sums = None
        for ch in range(SPAN_TOKENS // SUB):
            p, start = divmod(ch * SUB, HALF)
            rounded = []
            for b in range(SUB // TOK):
                shift = new + masked(stream, p, (start + b * TOK) // TOK)
                weights = jnp.exp2(now[pl.ds(ch * SUB + b * TOK, TOK), :] - shift)
                part = jnp.sum(weights.reshape(TOK // 8, 8, BQ), axis=0)
                sums = part if sums is None else sums + part
                rounded.append(weights.astype(jnp.bfloat16))
            product = jnp.dot(
                vt[stream, :, pl.ds(ch * SUB, SUB)], jnp.concatenate(rounded, axis=0), preferred_element_type=jnp.float32
            )
            update = product if update is None else update + product
        acc[block] = acc[block] * factor + update
        total[block] = total[block] * factor + sums
        last_one = jnp.where(windows == 0, (t >= QBLOCKS) & (t < 2 * QBLOCKS), (t >= 2 * QBLOCKS) & (stream == NEAR + ways - 1))

        @pl.when(last_one)
        def _():
            finish(block)

        return best

    take_kv(OWN, True)
    take_kv(OWN, False)
    take_q(jnp.int32(0))
    take_side(OWN)
    best = scores(jnp.int32(0), s0)

    def pair(i, best):
        best = step(2 * i, s0, s1, best)
        return step(2 * i + 1, s1, s0, best)

    lax.fori_loop(0, steps // 2, pair, best)

    columns = (SEQ - 1) * QW
    wait_bytes(out.at[0, :, pl.ds(0, QW)], out_local)
    wait_bytes(x.at[0, :, pl.ds(0, columns)], q_send)
    wait_bytes(x.at[0, :, pl.ds(0, 14 * HEAD_DIM)], kv_send.at[OWN])
    wait_bytes(x.at[0, :, pl.ds(0, 14 * HEAD_DIM)], kv_send.at[CACHE])
    for part in range(2):
        side_copy(OWN, part).wait_send()
        side_copy(CACHE, part).wait_send()

        @pl.when(c < SPANS - 1)
        def _():
            pass_copy(OWN, part).wait_send()

        @pl.when(c >= 1)
        def _():
            side_copy(NEAR, part).wait_send()

        @pl.when((c >= 1) & (c < SPANS - 1))
        def _():
            pass_copy(NEAR, part).wait_send()

        @pl.when(c >= 2)
        def _():
            side_copy(FAR, part).wait_send()

    wait_bytes(out.at[0, :, pl.ds(0, columns)], out_send)
    wait_bytes(out.at[0, :, pl.ds(0, columns)], out_recv)


def on_device(projected, cache_kv, levels, cache_blocks, gate_table):
    cache_rows = cache_kv.reshape(TOK, 2 * KV_WIDTH)
    dma = pltpu.SemaphoreType.DMA
    return pl.pallas_call(
        kernel,
        out_shape=jax.ShapeDtypeStruct((1, TOK, MODEL_WIDTH), jnp.bfloat16),
        in_specs=[
            pl.BlockSpec(memory_space=pl.ANY),
            pl.BlockSpec(memory_space=pl.ANY),
            pl.BlockSpec(memory_space=pltpu.SMEM),
            pl.BlockSpec(memory_space=pltpu.SMEM),
            pl.BlockSpec(memory_space=pltpu.VMEM),
        ],
        out_specs=pl.BlockSpec(memory_space=pl.ANY),
        scratch_shapes=[
            pltpu.VMEM((4, 2, 2, HALF, HEAD_DIM), jnp.bfloat16),
            pltpu.VMEM((4, HEAD_DIM, SPAN_TOKENS), jnp.bfloat16),
            pltpu.VMEM((SEQ, TOK, QW), jnp.bfloat16),
            pltpu.VMEM((QBLOCKS, 2 * HEAD_DIM, BQ), jnp.bfloat16),
            pltpu.VMEM((QBLOCKS, HEAD_DIM, BQ), jnp.float32),
            pltpu.VMEM((QBLOCKS, 8, BQ), jnp.float32),
            pltpu.VMEM((QBLOCKS, 8, BQ), jnp.float32),
            pltpu.VMEM((SPAN_TOKENS, BQ), jnp.float32),
            pltpu.VMEM((SPAN_TOKENS, BQ), jnp.float32),
            pltpu.VMEM((QBLOCKS, BQ, HEAD_DIM), jnp.bfloat16),
            pltpu.VMEM((8, QW), jnp.float32),
            dma((2,)), dma((2, 2)), dma((3,)), dma((4, 2)), dma((4, 2)), dma((2, 2)), dma((2, 2)),
            dma, dma((4,)), dma, dma, dma,
        ],
        compiler_params=pltpu.CompilerParams(
            collective_id=0, has_side_effects=True, vmem_limit_bytes=50 * 2**20
        ),
    )(projected, cache_rows, levels, cache_blocks, gate_table)


def solution(mesh):
    placed = (P("span", "seq", None), P("seq", None, None), P("span"), P("span"), P(None, "seq"))
    return jax.shard_map(
        on_device, mesh=mesh, in_specs=placed, out_specs=P("span", "seq", None), check_vma=False
    )
```

profile of v0, /device:TPU:7, one launch (start us, length us, event | category | flops | bytes accessed | tf_op | source)
XLA Modules:
  0.0 118.5 jit_solution(5782662850659226246)
XLA Ops:
  1.3 1.2 copy.6
  2.5 0.0 copy-start
  2.5 0.7 copy-done
  3.2 114.1 %shard_map.55 = bf16[1,128,6144]{2,1,0:T(8,128)(2,1)S(1)} custom-call(bf16[1,128,8192]{2,1,0:T(8,128)(2,1)} %x.1, bf16[128,2048]{1,0:T(8,128)(2,1)S(1)} %bitcast.2, s32[1]{0:T(128)S(6)} %copy.8.levels, s32[1]{0:T(128)S(6)} %copy.9.blocks, f32[16,384]{1,0:T(8,128)S(1)} %copy-done), custom_call_target="tpu_custom_call" | custom-call | tf_op jit(solution)/shard_map/pallas_call | solution.py:361
  117.3 1.1 copy.10
Async XLA Ops:
  2.5 0.7 copy-start
where the time goes:
time: 119 us; the launch traced here: 118 us
  Pallas kernels  114 us (96%)
  local copies, waits for them, and re-layouts  3.04 us (3%)
  between operations  1.32 us (1%)
    pallas_call x1, Pallas kernels, on_device(): pl.pallas_call(kernel, out_shape=jax.ShapeDtypeStruct((1, TOK, MODEL_WIDT...  114 us
    unnamed x4, local copies, waits for them, and re-layouts  3.04 us

commit v1 on v0

--- a/solution.py
+++ b/solution.py
@@ -20,23 +20,26 @@
 CHUNK = 512
 BQ = 512
 QBLOCKS = 12
-SUB = 512
+SUB = 256
 NEGATIVE = -1e30
 MASKED = 1e30
 SCALE = HEAD_DIM ** -0.5 * 1.4426950408889634
 OWN, CACHE, NEAR, FAR = range(4)
 MESH = pl.DeviceIdType.MESH
 
-CACHE_STEP = 7
-NEAR_STEPS = (6, 11)
-FAR_STEPS = (17, 22)
+CACHE_SENT = 11
+Q_SENT = ((1, 1, 1), (1, 2, 1), (3, 1, 2), (3, 2, 2), (5, 3, 0), (7, 3, 1), (9, 3, 2))
+CACHE_STEP = 19
+NEAR_STEPS = (6, 8)
+FAR_STEPS = (17, 21)
+EARLY_BLOCKS = 9
 
 
 def kernel(
     x, cache, levels, blocks, gate, out,
-    kv, vt, qin, qt, acc, top, total, s0, s1, stage, gates,
+    kv, vt, qin, qt, acc, top, total, s0, s1, stage, gates, gate_rows,
     kv_send, kv_recv, local_sem, side_send, side_recv, pass_send, pass_recv,
-    q_send, q_recv, out_send, out_recv, out_local,
+    q_send, q_recv, out_send, out_recv, out_local, gate_sem,
 ):
     c = lax.axis_index("span")
     s = lax.axis_index("seq")
@@ -47,10 +50,16 @@
     group = s // 4
     limit = blocks[0]
     windows = jnp.minimum(c, 2)
-    ways = jnp.maximum(windows, 1)
+    ways = jnp.where(c >= 2, 2, 1)
     steps = 2 * QBLOCKS + QBLOCKS * windows
+    closing = QBLOCKS + QBLOCKS * jnp.minimum(c, 1)
     beside = {"span": c, "seq": 2 * chip + (1 - core)}
-    after = {"span": jnp.minimum(c + 1, SPANS - 1), "seq": s}
+    flip = c // (SPANS // 2)
+    slot = (s + SEQ // 2 * flip) % SEQ
+    head_group = (chip + SEQ // 4 * flip) % (SEQ // 2)
+    across = (s + SEQ // 2) % SEQ
+    after = {"span": jnp.minimum(c + 1, SPANS - 1), "seq": jnp.where(c == SPANS // 2 - 1, across, s)}
+    before = {"span": jnp.maximum(c - 1, 0), "seq": jnp.where(c == SPANS // 2, across, s)}
 
     barrier = pltpu.get_barrier_semaphore()
     for d in range(1, SEQ):
@@ -58,12 +67,19 @@
 
     @pl.when(c > 0)
     def _():
-        pl.semaphore_signal(barrier, inc=1, device_id={"span": jnp.maximum(c - 1, 0), "seq": s}, device_id_type=MESH)
+        pl.semaphore_signal(barrier, inc=1, device_id=before, device_id_type=MESH)
 
     @pl.when(c < SPANS - 1)
     def _():
         pl.semaphore_signal(barrier, inc=1, device_id=after, device_id_type=MESH)
 
+    def clear(i, unused):
+        acc[i] = jnp.zeros((HEAD_DIM, BQ), jnp.float32)
+        total[i] = jnp.zeros((8, BQ), jnp.float32)
+        top[i] = jnp.full((8, BQ), NEGATIVE, jnp.float32)
+        return unused
+
+    lax.fori_loop(0, QBLOCKS, clear, 0)
     pl.semaphore_wait(barrier, SEQ - 1 + jnp.where(c > 0, 1, 0) + jnp.where(c < SPANS - 1, 1, 0))
 
     def source(stream, which, head):
@@ -77,7 +93,7 @@
             there = ((xlo + dx) % 2) * 4 + (y + dy) % 4
             for which in range(2):
                 pltpu.make_async_remote_copy(
-                    src_ref=source(stream, which, there),
+                    src_ref=source(stream, which, (there + SEQ // 4 * flip) % (SEQ // 2)),
                     dst_ref=kv.at[stream, core, which, piece],
                     send_sem=kv_send.at[stream],
                     recv_sem=kv_recv.at[stream, xlo],
@@ -85,44 +101,41 @@
                     device_id_type=MESH,
                 ).start()
         for which in range(2):
-            pltpu.make_async_copy(source(stream, which, chip), kv.at[stream, core, which, piece], local_sem.at[stream]).start()
+            pltpu.make_async_copy(source(stream, which, head_group), kv.at[stream, core, which, piece], local_sem.at[stream]).start()
 
     def group_at(turn):
         return ((group // 2 + turn // 2) % 2) * 2 + (group % 2 + turn % 2) % 2
 
-    def send_q(turn):
+    def send_q(turn, head):
         for e in range(4):
             there = 4 * group_at(turn) + (s % 4 + e) % 4
-            wanted = x.at[0, :, pl.ds(pl.multiple_of(QW * there, 128), QW)]
             if turn == 0 and e == 0:
-                pltpu.make_async_copy(wanted, qin.at[s], local_sem.at[2]).start()
-            else:
-                pltpu.make_async_remote_copy(
-                    src_ref=wanted,
-                    dst_ref=qin.at[s],
-                    send_sem=q_send,
-                    recv_sem=q_recv.at[group],
-                    device_id={"span": c, "seq": there},
-                    device_id_type=MESH,
-                ).start()
+                continue
+            pltpu.make_async_remote_copy(
+                src_ref=x.at[0, :, pl.ds(pl.multiple_of(QW * ((there + SEQ // 2 * flip) % SEQ) + HEAD_DIM * head, 128), HEAD_DIM)],
+                dst_ref=qin.at[s, :, pl.ds(HEAD_DIM * head, HEAD_DIM)],
+                send_sem=q_send,
+                recv_sem=q_recv.at[group, head],
+                device_id={"span": c, "seq": there},
+                device_id_type=MESH,
+            ).start()
+
+    gate_copy = pltpu.make_async_remote_copy(
+        src_ref=gate, dst_ref=gate_rows, send_sem=gate_sem.at[0], recv_sem=gate_sem.at[1],
+        device_id={"span": c, "seq": across}, device_id_type=MESH,
+    )
+
+    @pl.when(flip == 0)
+    def _():
+        pltpu.make_async_copy(gate, gate_rows, local_sem.at[3]).start()
+
+    @pl.when(flip == 1)
+    def _():
+        gate_copy.start()
 
     send_kv(OWN)
-    send_q(0)
-    send_q(1)
-    send_q(2)
-    send_kv(CACHE)
-    send_q(3)
-
-    def clear(i, unused):
-        acc[i] = jnp.zeros((HEAD_DIM, BQ), jnp.float32)
-        total[i] = jnp.zeros((8, BQ), jnp.float32)
-        top[i] = jnp.full((8, BQ), NEGATIVE, jnp.float32)
-        return unused
-
-    lax.fori_loop(0, QBLOCKS, clear, 0)
-    level_rows = lax.broadcasted_iota(jnp.int32, gate.shape, 0)
-    chosen = jnp.sum(jnp.where(level_rows == levels[0], gate[...], 0.0), axis=0, keepdims=True)
-    gates[...] = jnp.broadcast_to(chosen, gates.shape)
+    pltpu.make_async_copy(x.at[0, :, pl.ds(pl.multiple_of(QW * slot, 128), QW)], qin.at[s], local_sem.at[2]).start()
+    send_q(0, 0)
 
     def wait_bytes(ref, sem):
         pltpu.make_async_copy(ref, ref, sem).wait()
@@ -174,19 +187,28 @@
                 values = kv[stream, p, 1, pl.ds(b, 512), :]
                 vt[stream, :, pl.ds(p * HALF + b, 512)] = jnp.transpose(values)
 
+    def turn_of(i):
+        middle = (i >= HEADS) & (i < EARLY_BLOCKS)
+        turn = jnp.where(i < HEADS, 0, jnp.where(middle, 1 + (i - HEADS) % 2, 3))
+        head = jnp.where(i < HEADS, i, jnp.where(middle, (i - HEADS) // 2, i - EARLY_BLOCKS))
+        return turn, head
+
     def take_q(i):
-        g = group_at(i // HEADS)
+        turn, h = turn_of(i)
+        g = group_at(turn)
 
         @pl.when(i == 0)
         def _():
             wait_bytes(qin.at[0], local_sem.at[2])
-            wait_bytes(qin.at[pl.ds(0, 3)], q_recv.at[g])
-
-        @pl.when((i > 0) & (i % HEADS == 0))
-        def _():
-            wait_bytes(qin.at[pl.ds(0, 4)], q_recv.at[g])
-
-        h = i % HEADS
+
+        @pl.when(i < HEADS)
+        def _():
+            wait_bytes(qin.at[pl.ds(0, 3), :, pl.ds(0, HEAD_DIM)], q_recv.at[g, h])
+
+        @pl.when(i >= HEADS)
+        def _():
+            wait_bytes(qin.at[pl.ds(0, 4), :, pl.ds(0, HEAD_DIM)], q_recv.at[g, h])
+
         rows = qin[pl.ds(4 * g, 4), :, pl.ds(pl.multiple_of(h * HEAD_DIM, 128), HEAD_DIM)].reshape(BQ, HEAD_DIM)
         scaled = jnp.transpose(rows.astype(jnp.float32) * SCALE)
         high = scaled.astype(jnp.bfloat16)
@@ -194,38 +216,52 @@
         qt[i, pl.ds(128, 128), :] = (scaled - high.astype(jnp.float32)).astype(jnp.bfloat16)
 
     def place(t):
-        late = t - 2 * QBLOCKS
-        early = t < 2 * QBLOCKS
-        stream = jnp.where(early, t // QBLOCKS, NEAR + late % ways)
-        block = jnp.where(early, t % QBLOCKS, late // ways)
+        late = t - closing
+        once = 2 * EARLY_BLOCKS
+        rest = QBLOCKS - EARLY_BLOCKS
+        near = (c >= 1) & (((t >= EARLY_BLOCKS) & (t < once)) | (t >= once + rest))
+        skipped = jnp.where((c >= 1) & (t >= EARLY_BLOCKS), jnp.where(t >= once + rest, QBLOCKS, EARLY_BLOCKS), 0)
+        stream = jnp.where(late < 0, jnp.where(near, NEAR, OWN), jnp.where(late % ways == 0, CACHE, FAR))
+        block = jnp.where(late < 0, t - skipped, QBLOCKS - 1 - late // ways)
         return stream, block
 
     def masked(stream, p, piece):
         return jnp.where((stream == CACHE) & (2 * piece + p >= limit), MASKED, 0.0).astype(jnp.float32)
 
-    def scores(t, into):
-        stream, block = place(t)
-        queries = qt[block]
-        best = None
-        for ch in range(SPAN_TOKENS // SUB):
-            p, start = divmod(ch * SUB, HALF)
-            keys = kv[stream, p, 0, pl.ds(start, SUB), :]
-            part = jnp.dot(jnp.concatenate([keys, keys], axis=1), queries, preferred_element_type=jnp.float32)
-            into[pl.ds(ch * SUB, SUB), :] = part
-            for b in range(SUB // TOK):
-                here = jnp.max(part[b * TOK:(b + 1) * TOK].reshape(TOK // 8, 8, BQ), axis=0)
-                here = here - masked(stream, p, (start + b * TOK) // TOK)
-                best = here if best is None else jnp.maximum(best, here)
-        best = jnp.max(best, axis=0, keepdims=True)
+    def score_part(stream, queries, into, ch, best):
+        p, start = divmod(ch * SUB, HALF)
+        keys = kv[stream, p, 0, pl.ds(start, SUB), :]
+        part = jnp.dot(jnp.concatenate([keys, keys], axis=1), queries, preferred_element_type=jnp.float32)
+        into[pl.ds(ch * SUB, SUB), :] = part
+        for b in range(SUB // TOK):
+            here = jnp.max(part[b * TOK:(b + 1) * TOK].reshape(TOK // 8, 8, BQ), axis=0)
+            here = here - masked(stream, p, (start + b * TOK) // TOK)
+            best = here if best is None else jnp.maximum(best, here)
+        return best
+
+    def raised(block, best):
         old = top[block, 0:1, :]
-        return old, jnp.maximum(old, best)
+        return old, jnp.maximum(old, jnp.max(best, axis=0, keepdims=True))
 
     def arrivals(t):
-        @pl.when(t < QBLOCKS)
+        @pl.when((t < EARLY_BLOCKS) | ((c == 0) & (t < QBLOCKS)))
         def _():
             take_q(t)
 
-        @pl.when(t == CACHE_STEP)
+        @pl.when((c >= 1) & (t >= 2 * EARLY_BLOCKS) & (t < EARLY_BLOCKS + QBLOCKS))
+        def _():
+            take_q(t - EARLY_BLOCKS)
+
+        for at, turn, head in Q_SENT:
+            @pl.when(t == at)
+            def _(turn=turn, head=head):
+                send_q(turn, head)
+
+        @pl.when(t == CACHE_SENT)
+        def _():
+            send_kv(CACHE)
+
+        @pl.when(t == jnp.where(c == 0, QBLOCKS - 1, CACHE_STEP))
         def _():
             take_kv(CACHE, True)
             take_kv(CACHE, False)
@@ -240,15 +276,15 @@
             def _(which=which):
                 take_window(FAR, which == 0)
 
-        @pl.when(t == QBLOCKS)
+        @pl.when((t == EARLY_BLOCKS) & (c >= 1))
+        def _():
+            take_side(NEAR)
+
+        @pl.when(t == closing)
         def _():
             take_side(CACHE)
 
-        @pl.when((t == 2 * QBLOCKS) & (c >= 1))
-        def _():
-            take_side(NEAR)
-
-        @pl.when((t == 2 * QBLOCKS + 1) & (c >= 2))
+        @pl.when((t == closing + 1) & (c >= 2))
         def _():
             take_side(FAR)
 
@@ -257,11 +293,11 @@
         whole = jnp.sum(total[block], axis=0, keepdims=True)
         square = jnp.mean(summed * summed, axis=0, keepdims=True)
         normed = summed * lax.rsqrt(square + 1e-06 * (whole * whole))
-        h = block % HEADS
-        g = group_at(block // HEADS)
+        turn, h = turn_of(block)
+        g = group_at(turn)
         row = gates[0:1, pl.ds(pl.multiple_of(h * HEAD_DIM, 128), HEAD_DIM)]
         stage[block] = (jnp.transpose(normed) * row).astype(jnp.bfloat16)
-        wanted = out.at[0, :, pl.ds(pl.multiple_of((HEADS * s + h) * HEAD_DIM, 128), HEAD_DIM)]
+        wanted = out.at[0, :, pl.ds(pl.multiple_of((HEADS * slot + h) * HEAD_DIM, 128), HEAD_DIM)]
         for e in range(4):
             there = 4 * g + e
             held = stage.at[block, pl.ds(e * TOK, TOK)]
@@ -281,17 +317,19 @@
         old, new = best
         stream, block = place(t)
         top[block, 0:1, :] = new
-        following = jnp.minimum(t + 1, steps - 1)
 
         @pl.when(t + 1 < steps)
         def _():
             arrivals(t + 1)
 
-        best = scores(following, later)
+        next_stream, next_block = place(jnp.minimum(t + 1, steps - 1))
+        queries = qt[next_block]
         factor = jnp.exp2(old - new)
+        best = None
         update = None
         sums = None
         for ch in range(SPAN_TOKENS // SUB):
+            best = score_part(next_stream, queries, later, ch, best)
             p, start = divmod(ch * SUB, HALF)
             rounded = []
             for b in range(SUB // TOK):
@@ -306,19 +344,37 @@
             update = product if update is None else update + product
         acc[block] = acc[block] * factor + update
         total[block] = total[block] * factor + sums
-        last_one = jnp.where(windows == 0, (t >= QBLOCKS) & (t < 2 * QBLOCKS), (t >= 2 * QBLOCKS) & (stream == NEAR + ways - 1))
-
-        @pl.when(last_one)
+
+        @pl.when((t >= closing) & ((t - closing) % ways == ways - 1))
         def _():
             finish(block)
 
-        return best
+        return raised(next_block, best)
+
+    @pl.when(flip == 0)
+    def _():
+        pltpu.make_async_copy(gate, gate_rows, local_sem.at[3]).wait()
+
+    @pl.when(flip == 1)
+    def _():
+        gate_copy.wait()
+
+    level_rows = lax.broadcasted_iota(jnp.int32, gate_rows.shape, 0)
+    chosen = jnp.sum(jnp.where(level_rows == levels[0], gate_rows[...], 0.0), axis=0, keepdims=True)
+    gates[...] = jnp.broadcast_to(chosen, gates.shape)
 
     take_kv(OWN, True)
+    send_q(0, 1)
+    send_q(0, 2)
     take_kv(OWN, False)
+    send_q(1, 0)
+    send_q(2, 0)
     take_q(jnp.int32(0))
     take_side(OWN)
-    best = scores(jnp.int32(0), s0)
+    best = None
+    for ch in range(SPAN_TOKENS // SUB):
+        best = score_part(OWN, qt[0], s0, ch, best)
+    best = raised(0, best)
 
     def pair(i, best):
         best = step(2 * i, s0, s1, best)
@@ -366,7 +422,7 @@
             pl.BlockSpec(memory_space=pl.ANY),
             pl.BlockSpec(memory_space=pltpu.SMEM),
             pl.BlockSpec(memory_space=pltpu.SMEM),
-            pl.BlockSpec(memory_space=pltpu.VMEM),
+            pl.BlockSpec(memory_space=pl.ANY),
         ],
         out_specs=pl.BlockSpec(memory_space=pl.ANY),
         scratch_shapes=[
@@ -381,8 +437,9 @@
             pltpu.VMEM((SPAN_TOKENS, BQ), jnp.float32),
             pltpu.VMEM((QBLOCKS, BQ, HEAD_DIM), jnp.bfloat16),
             pltpu.VMEM((8, QW), jnp.float32),
-            dma((2,)), dma((2, 2)), dma((3,)), dma((4, 2)), dma((4, 2)), dma((2, 2)), dma((2, 2)),
-            dma, dma((4,)), dma, dma, dma,
+            pltpu.VMEM((16, QW), jnp.float32),
+            dma((2,)), dma((2, 2)), dma((4,)), dma((4, 2)), dma((4, 2)), dma((2, 2)), dma((2, 2)),
+            dma, dma((4, 3)), dma, dma, dma, dma((2,)),
         ],
         compiler_params=pltpu.CompilerParams(
             collective_id=0, has_side_effects=True, vmem_limit_bytes=50 * 2**20

time: 119 us -> 94.7 us (0.80); the launches traced: 118 us -> 92.9 us
  Pallas kernels: 114 us -> 88.5 us
    pallas_call x1, Pallas kernels: 114 us -> 88.5 us  [on_device(): pl.pallas_call(kernel, out_shape=jax.ShapeDtypeStruct((1, TOK, MODEL_WIDT...]
where the time goes in v1:
time: 94.7 us; the launch traced here: 92.9 us
  Pallas kernels  88.5 us (93%)
  local copies, waits for them, and re-layouts  3.04 us (3%)
  between operations  1.32 us (1%)
    pallas_call x1, Pallas kernels, on_device(): pl.pallas_call(kernel, out_shape=jax.ShapeDtypeStruct((1, TOK, MODEL_WIDT...  88.5 us
    unnamed x4, local copies, waits for them, and re-layouts  3.04 us

profile of v1, /device:TPU:7, one launch (start us, length us, event | category | flops | bytes accessed | tf_op | source)
XLA Modules:
  0.0 92.9 jit_solution(10288665750399488196)
XLA Ops:
  1.3 1.2 %copy.6 = bf16[16,8,2,1024]{3,1,2,0:T(8,128)(2,1)S(1)} copy(bf16[16,8,2,1024]{3,2,1,0:T(2,128)(2,1)} %bitcast.3) | data formatting | bytes 1048576
  2.5 0.0 copy-start
  2.5 0.7 copy-done
  3.2 88.5 %shard_map.55 = bf16[1,128,6144]{2,1,0:T(8,128)(2,1)S(1)} custom-call(bf16[1,128,8192]{2,1,0:T(8,128)(2,1)} %x.1, bf16[128,2048]{1,0:T(8,128)(2,1)S(1)} %bitcast.2, s32[1]{0:T(128)S(6)} %copy.8.levels, s32[1]{0:T(128)S(6)} %copy.9.blocks, f32[16,384]{1,0:T(8,128)S(1)} %copy-done), custom_call_target="tpu_custom_call" | custom-call | tf_op jit(solution)/shard_map/pallas_call | solution.py:417
  91.7 1.1 %copy.10 = bf16[1,128,6144]{2,1,0:T(8,128)(2,1)} copy(bf16[1,128,6144]{2,1,0:T(8,128)(2,1)S(1)} %shard_map.55) | data formatting | bytes 3145728
Async XLA Ops:
  2.5 0.7 copy-start

commit v2 on v1

--- a/solution.py
+++ b/solution.py
@@ -73,6 +73,18 @@
     def _():
         pl.semaphore_signal(barrier, inc=1, device_id=after, device_id_type=MESH)
 
+    def source(stream, which, head):
+        if stream == OWN:
+            return x.at[0, :, pl.ds(pl.multiple_of(MODEL_WIDTH + KV_WIDTH * which + HEAD_DIM * head, 128), HEAD_DIM)]
+        return cache.at[:, pl.ds(pl.multiple_of(KV_WIDTH * which + HEAD_DIM * head, 128), HEAD_DIM)]
+
+    piece = pl.ds(pl.multiple_of(TOK * chip, TOK), TOK)
+
+    for stream in (OWN, CACHE):
+        for which in range(2):
+            pltpu.make_async_copy(source(stream, which, head_group), kv.at[stream, core, which, piece], local_sem.at[stream]).start()
+    pltpu.make_async_copy(x.at[0, :, pl.ds(pl.multiple_of(QW * slot, 128), QW)], qin.at[s], local_sem.at[2]).start()
+
     def clear(i, unused):
         acc[i] = jnp.zeros((HEAD_DIM, BQ), jnp.float32)
         total[i] = jnp.zeros((8, BQ), jnp.float32)
@@ -82,13 +94,7 @@
     lax.fori_loop(0, QBLOCKS, clear, 0)
     pl.semaphore_wait(barrier, SEQ - 1 + jnp.where(c > 0, 1, 0) + jnp.where(c < SPANS - 1, 1, 0))
 
-    def source(stream, which, head):
-        if stream == OWN:
-            return x.at[0, :, pl.ds(pl.multiple_of(MODEL_WIDTH + KV_WIDTH * which + HEAD_DIM * head, 128), HEAD_DIM)]
-        return cache.at[:, pl.ds(pl.multiple_of(KV_WIDTH * which + HEAD_DIM * head, 128), HEAD_DIM)]
-
     def send_kv(stream):
-        piece = pl.ds(pl.multiple_of(TOK * chip, TOK), TOK)
         for dx, dy in ((0, 1), (0, 3), (0, 2), (1, 0), (1, 1), (1, 3), (1, 2)):
             there = ((xlo + dx) % 2) * 4 + (y + dy) % 4
             for which in range(2):
@@ -100,8 +106,6 @@
                     device_id={"span": c, "seq": 2 * there + core},
                     device_id_type=MESH,
                 ).start()
-        for which in range(2):
-            pltpu.make_async_copy(source(stream, which, head_group), kv.at[stream, core, which, piece], local_sem.at[stream]).start()
 
     def group_at(turn):
         return ((group // 2 + turn // 2) % 2) * 2 + (group % 2 + turn % 2) % 2
@@ -134,7 +138,6 @@
         gate_copy.start()
 
     send_kv(OWN)
-    pltpu.make_async_copy(x.at[0, :, pl.ds(pl.multiple_of(QW * slot, 128), QW)], qin.at[s], local_sem.at[2]).start()
     send_q(0, 0)
 
     def wait_bytes(ref, sem):
@@ -179,13 +182,16 @@
             def _():
                 pass_copy(NEAR, part).start()
 
+    def turn_values(stream, p):
+        for b in range(0, HALF, 512):
+            columns = pl.ds(pl.multiple_of(p * HALF + b, 512), 512)
+            vt[stream, :, columns] = jnp.transpose(kv[stream, p, 1, pl.ds(b, 512), :])
+
     def take_side(stream):
+        turn_values(stream, core)
         for part in range(2):
             wait_bytes(kv.at[stream, 1 - core, :, pl.ds(0, CHUNK)], side_recv.at[stream, part])
-        for p in range(2):
-            for b in range(0, HALF, 512):
-                values = kv[stream, p, 1, pl.ds(b, 512), :]
-                vt[stream, :, pl.ds(p * HALF + b, 512)] = jnp.transpose(values)
+        turn_values(stream, 1 - core)
 
     def turn_of(i):
         middle = (i >= HEADS) & (i < EARLY_BLOCKS)
@@ -210,7 +216,7 @@
             wait_bytes(qin.at[pl.ds(0, 4), :, pl.ds(0, HEAD_DIM)], q_recv.at[g, h])
 
         rows = qin[pl.ds(4 * g, 4), :, pl.ds(pl.multiple_of(h * HEAD_DIM, 128), HEAD_DIM)].reshape(BQ, HEAD_DIM)
-        scaled = jnp.transpose(rows.astype(jnp.float32) * SCALE)
+        scaled = jnp.transpose(rows).astype(jnp.float32) * SCALE
         high = scaled.astype(jnp.bfloat16)
         qt[i, pl.ds(0, 128), :] = high
         qt[i, pl.ds(128, 128), :] = (scaled - high.astype(jnp.float32)).astype(jnp.bfloat16)
@@ -295,8 +301,8 @@
         normed = summed * lax.rsqrt(square + 1e-06 * (whole * whole))
         turn, h = turn_of(block)
         g = group_at(turn)
-        row = gates[0:1, pl.ds(pl.multiple_of(h * HEAD_DIM, 128), HEAD_DIM)]
-        stage[block] = (jnp.transpose(normed) * row).astype(jnp.bfloat16)
+        scale = jnp.concatenate([gates[h]] * (BQ // HEAD_DIM), axis=1)
+        stage[block] = jnp.transpose((normed * scale).astype(jnp.bfloat16))
         wanted = out.at[0, :, pl.ds(pl.multiple_of((HEADS * slot + h) * HEAD_DIM, 128), HEAD_DIM)]
         for e in range(4):
             there = 4 * g + e
@@ -313,23 +319,22 @@
                     device_id={"span": c, "seq": there}, device_id_type=MESH,
                 ).start()
 
-    def step(t, now, later, best):
+    def step(t, now, later, best, last=False):
         old, new = best
         stream, block = place(t)
         top[block, 0:1, :] = new
 
-        @pl.when(t + 1 < steps)
-        def _():
+        if not last:
             arrivals(t + 1)
-
-        next_stream, next_block = place(jnp.minimum(t + 1, steps - 1))
-        queries = qt[next_block]
+            next_stream, next_block = place(t + 1)
+            queries = qt[next_block]
         factor = jnp.exp2(old - new)
         best = None
         update = None
         sums = None
         for ch in range(SPAN_TOKENS // SUB):
-            best = score_part(next_stream, queries, later, ch, best)
+            if not last:
+                best = score_part(next_stream, queries, later, ch, best)
             p, start = divmod(ch * SUB, HALF)
             rounded = []
             for b in range(SUB // TOK):
@@ -349,7 +354,7 @@
         def _():
             finish(block)
 
-        return raised(next_block, best)
+        return None if last else raised(next_block, best)
 
     @pl.when(flip == 0)
     def _():
@@ -361,7 +366,8 @@
 
     level_rows = lax.broadcasted_iota(jnp.int32, gate_rows.shape, 0)
     chosen = jnp.sum(jnp.where(level_rows == levels[0], gate_rows[...], 0.0), axis=0, keepdims=True)
-    gates[...] = jnp.broadcast_to(chosen, gates.shape)
+    for h in range(HEADS):
+        gates[h] = jnp.transpose(jnp.broadcast_to(chosen[:, h * HEAD_DIM:(h + 1) * HEAD_DIM], (HEAD_DIM, HEAD_DIM)))
 
     take_kv(OWN, True)
     send_q(0, 1)
@@ -380,7 +386,9 @@
         best = step(2 * i, s0, s1, best)
         return step(2 * i + 1, s1, s0, best)
 
-    lax.fori_loop(0, steps // 2, pair, best)
+    best = lax.fori_loop(0, steps // 2 - 1, pair, best)
+    best = step(steps - 2, s0, s1, best)
+    step(steps - 1, s1, s0, best, last=True)
 
     columns = (SEQ - 1) * QW
     wait_bytes(out.at[0, :, pl.ds(0, QW)], out_local)
@@ -436,7 +444,7 @@
             pltpu.VMEM((SPAN_TOKENS, BQ), jnp.float32),
             pltpu.VMEM((SPAN_TOKENS, BQ), jnp.float32),
             pltpu.VMEM((QBLOCKS, BQ, HEAD_DIM), jnp.bfloat16),
-            pltpu.VMEM((8, QW), jnp.float32),
+            pltpu.VMEM((HEADS, HEAD_DIM, HEAD_DIM), jnp.float32),
             pltpu.VMEM((16, QW), jnp.float32),
             dma((2,)), dma((2, 2)), dma((4,)), dma((4, 2)), dma((4, 2)), dma((2, 2)), dma((2, 2)),
             dma, dma((4, 3)), dma, dma, dma, dma((2,)),

time: 94.7 us -> 92.8 us (0.980)
  Pallas kernels: 88.5 us -> 86.7 us
    pallas_call x1, Pallas kernels: 88.5 us -> 86.7 us  [on_device(): pl.pallas_call(kernel, out_shape=jax.ShapeDtypeStruct((1, TOK, MODEL_WIDT...]
where the time goes in v2:
time: 92.8 us; the launch traced here: 91 us
  Pallas kernels  86.7 us (93%)
  local copies, waits for them, and re-layouts  3.04 us (3%)
  between operations  1.32 us (1%)
    pallas_call x1, Pallas kernels, on_device(): pl.pallas_call(kernel, out_shape=jax.ShapeDtypeStruct((1, TOK, MODEL_WIDT...  86.7 us
    unnamed x4, local copies, waits for them, and re-layouts  3.04 us

profile of v2, /device:TPU:7, one launch (start us, length us, event | category | flops | bytes accessed | tf_op | source)
XLA Modules:
  0.0 91.0 jit_solution(18326743797185899210)
XLA Ops:
  1.3 1.2 %copy.6 = bf16[16,8,2,1024]{3,1,2,0:T(8,128)(2,1)S(1)} copy(bf16[16,8,2,1024]{3,2,1,0:T(2,128)(2,1)} %bitcast.3) | data formatting | bytes 1048576
  2.5 0.0 copy-start
  2.5 0.7 copy-done
  3.2 86.7 %shard_map.55 = bf16[1,128,6144]{2,1,0:T(8,128)(2,1)S(1)} custom-call(bf16[1,128,8192]{2,1,0:T(8,128)(2,1)} %x.1, bf16[128,2048]{1,0:T(8,128)(2,1)S(1)} %bitcast.2, s32[1]{0:T(128)S(6)} %copy.8.levels, s32[1]{0:T(128)S(6)} %copy.9.blocks, f32[16,384]{1,0:T(8,128)S(1)} %copy-done), custom_call_target="tpu_custom_call" | custom-call | tf_op jit(solution)/shard_map/pallas_call | solution.py:425
  89.9 1.1 %copy.10 = bf16[1,128,6144]{2,1,0:T(8,128)(2,1)} copy(bf16[1,128,6144]{2,1,0:T(8,128)(2,1)S(1)} %shard_map.55) | data formatting | bytes 3145728
Async XLA Ops:
  2.5 0.7 copy-start

commit v3 on v2

--- a/solution.py
+++ b/solution.py
@@ -28,7 +28,7 @@
 MESH = pl.DeviceIdType.MESH
 
 CACHE_SENT = 11
-Q_SENT = ((1, 1, 1), (1, 2, 1), (3, 1, 2), (3, 2, 2), (5, 3, 0), (7, 3, 1), (9, 3, 2))
+Q_SENT = ((1, 1, 1), (1, 2, 1), (3, 1, 2), (3, 2, 2), (6, 3, 0), (7, 3, 1), (8, 3, 2))
 CACHE_STEP = 19
 NEAR_STEPS = (6, 8)
 FAR_STEPS = (17, 21)

time: 92.8 us -> 90.9 us (0.980); the launches traced: 91 us -> 90.7 us
  no operation moved by 1% of the time
where the time goes in v3:
time: 90.9 us; the launch traced here: 90.7 us
  Pallas kernels  86.3 us (95%)
  local copies, waits for them, and re-layouts  3.04 us (3%)
  between operations  1.32 us (1%)
    pallas_call x1, Pallas kernels, on_device(): pl.pallas_call(kernel, out_shape=jax.ShapeDtypeStruct((1, TOK, MODEL_WIDT...  86.3 us
    unnamed x4, local copies, waits for them, and re-layouts  3.04 us

profile of v3, /device:TPU:7, one launch (start us, length us, event | category | flops | bytes accessed | tf_op | source)
XLA Modules:
  0.0 90.7 jit_solution(16024220567378520050)
XLA Ops:
  1.3 1.2 %copy.6 = bf16[16,8,2,1024]{3,1,2,0:T(8,128)(2,1)S(1)} copy(bf16[16,8,2,1024]{3,2,1,0:T(2,128)(2,1)} %bitcast.3) | data formatting | bytes 1048576
  2.5 0.0 copy-start
  2.5 0.7 copy-done
  3.2 86.3 %shard_map.55 = bf16[1,128,6144]{2,1,0:T(8,128)(2,1)S(1)} custom-call(bf16[1,128,8192]{2,1,0:T(8,128)(2,1)} %x.1, bf16[128,2048]{1,0:T(8,128)(2,1)S(1)} %bitcast.2, s32[1]{0:T(128)S(6)} %copy.8.levels, s32[1]{0:T(128)S(6)} %copy.9.blocks, f32[16,384]{1,0:T(8,128)S(1)} %copy-done), custom_call_target="tpu_custom_call" | custom-call | tf_op jit(solution)/shard_map/pallas_call | solution.py:425
  89.5 1.1 %copy.10 = bf16[1,128,6144]{2,1,0:T(8,128)(2,1)} copy(bf16[1,128,6144]{2,1,0:T(8,128)(2,1)S(1)} %shard_map.55) | data formatting | bytes 3145728
Async XLA Ops:
  2.5 0.7 copy-start
